TPU v7x, 32 devices: a whole 2x2x4 slice. The times are simulated.
32 devices in a mesh: rad: 4 (over y, core), ax: 8 (over z, x).
Axes of the slice: x: 2, y: 2, z: 4, core: 2. Of those that a mesh axis runs over, the one named last changes fastest.
Arguments:
- charge: float32 [64, 128, 128], P('rad', 'ax'), may hold values from -6 to 6
- density: float32 [64, 128, 128], P('rad', 'ax'), may hold values from 0.1 to 20
- previous: float32 [64, 128, 128], P('rad', 'ax'), may hold values from -4 to 4
- levels: int32 [4, 8, 8], P('rad', 'ax'), may hold values from 0 to 2
Outputs:
- potential: float32 [64, 128, 128], P('rad', 'ax')
All inputs are finite; a program needn't handle non-finite values.
Results may differ from a plain program's by a relative error of at most 0.0003.
Values sent between devices are 32-bit elements; how exact they have to be, the bound alone decides.
A program may use at most 64 MiB of HBM per device.

v0:
```python
import jax
import jax.numpy as jnp
from jax import lax
from jax.experimental import pallas as pl
from jax.experimental.pallas import tpu as pltpu
from jax.sharding import PartitionSpec as P

NU = 2
EXTRA = 2
CS = 8
PATCH = 16
MESH = pl.DeviceIdType.MESH
NX = 24


def make_kernel(nrad, nax):
    nd = nrad * nax

    def kernel(charge, density, previous, levels, out, v, e, co, g0, d0, tmp, src1, m, e1, co1, g1, d1,
               st, hal, gat, eg, cg, sg, f2, send_sem, recv_sem, gsend, grecv):
        R, A, W = 16, 16, 128
        ri, ai = lax.axis_index("rad"), lax.axis_index("ax")
        me = ri * nax + ai
        has = (ri > 0, ri < nrad - 1, ai > 0, ai < nax - 1)
        nbr = ((ri - 1, ai), (ri + 1, ai), (ri, ai - 1), (ri, ai + 1))
        opp = (1, 0, 3, 2)

        barrier = pltpu.get_barrier_semaphore()

        def greet(i, c):
            @pl.when(i != me)
            def _():
                pl.semaphore_signal(barrier, inc=1, device_id=(i // nax, i % nax), device_id_type=MESH)
            return c

        lax.fori_loop(0, nd, greet, 0)
        zero = jnp.zeros((16, 128), jnp.float32)
        for d in range(4):
            @pl.when(jnp.logical_not(has[d]))
            def _(d=d):
                for x in range(NX):
                    hal[x, d] = zero

        def copy(x, d, n, to_slot):
            return pltpu.make_async_remote_copy(
                src_ref=st.at[x, d, pl.ds(0, n)], dst_ref=hal.at[x, to_slot, pl.ds(0, n)],
                send_sem=send_sem.at[x, d], recv_sem=recv_sem.at[x, to_slot],
                device_id=nbr[d], device_id_type=MESH)

        used = {}

        def send(x, ref, n):
            used[x] = n
            st[x, 0, 0:n] = ref[1]
            st[x, 1, 0:n] = ref[n]
            st[x, 2, 0:n] = ref[1:n + 1, 0, :]
            st[x, 3, 0:n] = ref[1:n + 1, n - 1, :]
            for d in range(4):
                @pl.when(has[d])
                def _(d=d):
                    copy(x, d, n, opp[d]).start()

        def recv(x, ref, n):
            for d in range(4):
                @pl.when(has[d])
                def _(d=d):
                    copy(x, d, n, d).wait_recv()
            ref[0] = hal[x, 0, 0:n]
            ref[n + 1] = hal[x, 1, 0:n]

        def shifts(ref, x, r, n, step):
            c = ref[r + 1]
            sub = lax.broadcasted_iota(jnp.int32, (n, 128), 0)
            left = pltpu.roll(c, 1, 0)
            right = pltpu.roll(c, n - 1, 0)
            hl = 0.0 if x is None else hal[x, 2, r:r + 1]
            hr = 0.0 if x is None else hal[x, 3, r:r + 1]
            left = jnp.where(sub == 0, hl, left)
            right = jnp.where(sub == n - 1, hr, right)
            return c, (ref[r], ref[r + 2], left, right, pltpu.roll(c, step, 1), pltpu.roll(c, 128 - step, 1))

        def coefs(ref, x, n, step, scale, cref, gref, dref, source):
            lane = lax.broadcasted_iota(jnp.int32, (n, 128), 1)
            for r in range(n):
                c, (u, dn, l, rt, wl, wr) = shifts(ref, x, r, n, step)
                wl = jnp.where(lane < step, 0.0, wl)
                wr = jnp.where(lane >= 128 - step, 0.0, wr)
                diag = (6.0 * c + u + dn + l + rt + wl + wr) * (0.5 * scale)
                inv = 1.0 / diag
                h = inv * (0.5 * scale)
                cref[0, r] = (c + u) * h
                cref[1, r] = (c + dn) * h
                cref[2, r] = (c + l) * h
                cref[3, r] = (c + rt) * h
                cref[4, r] = jnp.where(lane < step, 0.0, (c + wl) * h)
                cref[5, r] = jnp.where(lane >= 128 - step, 0.0, (c + wr) * h)
                dref[r] = diag
                if source is not None:
                    gref[r] = source[r] * inv

        def update(ref, x, r, n, step, cref, gref):
            c, nb = shifts(ref, x, r, n, step)
            t = (gref[r] + cref[0, r] * nb[0]) + cref[1, r] * nb[1]
            s = cref[2, r] * nb[2] + cref[3, r] * nb[3]
            q = cref[4, r] * nb[4] + cref[5, r] * nb[5]
            return c, t + (s + q)

        def parity_of(n, step):
            return (lax.broadcasted_iota(jnp.int32, (n, 128), 0)
                    + lax.broadcasted_iota(jnp.int32, (n, 128), 1) // step) % 2

        def half(ref, x, n, step, cref, gref, colour, mask=None):
            par = parity_of(n, step)
            ms = [par == colour, par == 1 - colour]
            if mask is not None:
                ms = [jnp.logical_and(k, mask) for k in ms]
            for r in range(n):
                c, new = update(ref, x, r, n, step, cref, gref)
                ref[r + 1] = jnp.where(ms[r % 2], new, c)

        for r in range(R):
            e[r + 1] = 1.0 + 0.5 * density[r]
            v[r + 1] = previous[r]
        pl.semaphore_wait(barrier, nd - 1)
        send(0, e, R)
        send(1, v, R)
        lane16 = lax.broadcasted_iota(jnp.int32, (16, 128), 1)
        lev = jnp.zeros((16, 128), jnp.int32)
        for p in range(8):
            lev = jnp.where(lane16 // PATCH == p, levels[0, 0, p], lev)

        lane8 = lax.broadcasted_iota(jnp.int32, (8, 128), 1)
        sub8 = lax.broadcasted_iota(jnp.int32, (8, 128), 0)

        def pairs(x, lane, w):
            n = x.shape[0]
            return x + jnp.where(lane % (2 * w) < w, pltpu.roll(x, 128 - w, 1), pltpu.roll(x, w, 1))

        for q in range(8):
            tmp[q] = e[2 * q + 1] + e[2 * q + 2]
        for q in range(8):
            s = tmp[q, pl.ds(0, 8, stride=2), :] + tmp[q, pl.ds(1, 8, stride=2), :]
            e1[q + 1] = pairs(s, lane8, 1) * 0.125
        send(2, e1, 8)

        recv(0, e, R)
        coefs(e, 0, R, 1, 1.0, co, g0, d0, charge)
        recv(1, v, R)
        x = 1
        nxt = 3
        for sweep in range(NU + EXTRA):
            mask = None if sweep < NU else lev > (sweep - NU)
            for colour in range(2):
                half(v, x, R, 1, co, g0, colour, mask)
                x = nxt
                nxt += 1
                send(x, v, R)
                if sweep == 0 and colour == 0:
                    recv(2, e1, 8)
                    coefs(e1, 2, 8, 2, 0.25, co1, None, d1, None)
                recv(x, v, R)
        for q in range(8):
            rs = []
            for r in (2 * q, 2 * q + 1):
                c, new = update(v, x, r, R, 1, co, g0)
                rs.append(d0[r] * (new - c))
            tmp[q] = rs[0] + rs[1]
        for q in range(8):
            s = tmp[q, pl.ds(0, 8, stride=2), :] + tmp[q, pl.ds(1, 8, stride=2), :]
            g1[q] = pairs(s, lane8, 1) * 0.125 / d1[q]
        par = parity_of(8, 2)
        m[0] = zero[:8]
        m[9] = zero[:8]
        for r in range(8):
            m[r + 1] = jnp.where(par == r % 2, g1[r], 0.0)
        for i in range(1, 2 * NU + 1):
            x = nxt
            nxt += 1
            send(x, m, 8)
            recv(x, m, 8)
            if i < 2 * NU:
                half(m, x, 8, 2, co1, g1, i % 2)
        for q in range(4):
            rs = []
            for r in (2 * q, 2 * q + 1):
                c, new = update(m, x, r, 8, 2, co1, g1)
                rs.append(d1[r] * (new - c))
            tmp[q, 0:8] = rs[0] + rs[1]
            tmp[q, 8:16] = e1[2 * q + 1] + e1[2 * q + 2]
        lane1 = lax.broadcasted_iota(jnp.int32, (1, 128), 1)
        for k in range(2):
            for q in range(4):
                y = tmp[q, 8 * k:8 * k + 8]
                y = pairs(y, lane8, 2)
                tmp[q, 8 * k:8 * k + 8] = y
        for k in range(2):
            for q in range(4):
                p = jnp.zeros((1, 128), jnp.float32)
                for j in range(4):
                    a = 8 * k + 2 * j
                    p = jnp.where(lane1 % 4 == j, tmp[q, a:a + 1] + tmp[q, a + 1:a + 2], p)
                gat[me, pl.ds(4 * k + q, 1)] = p * 0.125

        def gcopy(i):
            return pltpu.make_async_remote_copy(
                src_ref=gat.at[me], dst_ref=gat.at[me], send_sem=gsend, recv_sem=grecv,
                device_id=(i // nax, i % nax), device_id_type=MESH)

        def scatter(i, c):
            @pl.when(i != me)
            def _():
                gcopy(i).start()
            return c

        lax.fori_loop(0, nd, scatter, 0)
        pltpu.make_async_remote_copy(
            src_ref=gat.at[pl.ds(0, nd - 1)], dst_ref=gat.at[pl.ds(0, nd - 1)], send_sem=gsend, recv_sem=grecv,
            device_id=nbr[0], device_id_type=MESH).wait_recv()

        n2 = nrad * 4
        zc = jnp.zeros((nax, 128), jnp.float32)
        sub = lax.broadcasted_iota(jnp.int32, (nax, 128), 0)
        lane = lax.broadcasted_iota(jnp.int32, (nax, 128), 1)
        j4 = lane % 4

        def around(c):
            lf = jnp.where(j4 == 0, pltpu.roll(pltpu.roll(c, 125, 1), 1, 0), pltpu.roll(c, 1, 1))
            rt = jnp.where(j4 == 3, pltpu.roll(pltpu.roll(c, 3, 1), nax - 1, 0), pltpu.roll(c, 127, 1))
            return lf, rt, pltpu.roll(c, 4, 1), pltpu.roll(c, 124, 1)

        first = jnp.logical_and(sub == 0, j4 == 0)
        last = jnp.logical_and(sub == nax - 1, j4 == 3)
        low = lane < 4
        high = lane >= 124
        eg[0] = zc
        eg[n2 + 1] = zc
        f2[0] = zc
        f2[n2 + 1] = zc
        for r in range(n2):
            eg[r + 1] = gat[(r // 4) * nax:(r // 4 + 1) * nax, 4 + r % 4, :]
            f2[r + 1] = zc

        def coarse_coefs(r, _):
            c = eg[r + 1]
            lf, rt, wl, wr = around(c)
            lf = jnp.where(first, 0.0, lf)
            rt = jnp.where(last, 0.0, rt)
            wl = jnp.where(low, 0.0, wl)
            wr = jnp.where(high, 0.0, wr)
            u, dn = eg[r], eg[r + 2]
            t = 6.0 * c + u + dn + lf + rt + wl + wr
            h = 1.0 / t
            cg[0, r] = (c + u) * h
            cg[1, r] = (c + dn) * h
            cg[2, r] = jnp.where(first, 0.0, (c + lf) * h)
            cg[3, r] = jnp.where(last, 0.0, (c + rt) * h)
            cg[4, r] = jnp.where(low, 0.0, (c + wl) * h)
            cg[5, r] = jnp.where(high, 0.0, (c + wr) * h)
            sg[r] = h * 32.0
            return 0

        for r in range(n2):
            coarse_coefs(r, 0)
            sg[r] = sg[r] * gat[(r // 4) * nax:(r // 4 + 1) * nax, r % 4, :]
        par2 = (j4 + lane // 4) % 2

        def coarse_sweep(k, _):
            for colour in range(2):
                for r in range(n2):
                    c = f2[r + 1]
                    lf, rt, wl, wr = around(c)
                    t = sg[r] + cg[0, r] * f2[r] + cg[1, r] * f2[r + 2]
                    t = t + (cg[2, r] * lf + cg[3, r] * rt) + (cg[4, r] * wl + cg[5, r] * wr)
                    f2[r + 1] = jnp.where(par2 == (colour + r) % 2, t, c)
            return 0

        lax.fori_loop(0, CS, coarse_sweep, 0)

        m4 = lane8 % 4
        for q in range(4):
            own = jnp.broadcast_to(f2[4 * ri + q + 1, pl.ds(ai, 1), :], (8, 128))
            t = jnp.zeros((8, 128), jnp.float32)
            want = sub8 // 2 - m4
            for s in range(-3, 4):
                t = jnp.where(want == s, own if s == 0 else pltpu.roll(own, (-s) % 128, 1), t)
            m[2 * q + 1] = m[2 * q + 1] + t
            m[2 * q + 2] = m[2 * q + 2] + t
        for i in range(2 * NU):
            x = nxt
            nxt += 1
            send(x, m, 8)
            recv(x, m, 8)
            half(m, x, 8, 2, co1, g1, i % 2)
        for q in range(8):
            y = m[q + 1]
            tmp[q, pl.ds(0, 8, stride=2), :] = y
            tmp[q, pl.ds(1, 8, stride=2), :] = y
        for r in range(R):
            v[r + 1] = v[r + 1] + tmp[r // 2]
        for i in range(2 * NU):
            x = nxt
            nxt += 1
            send(x, v, R)
            recv(x, v, R)
            half(v, x, R, 1, co, g0, i % 2)
        out[...] = v[1:R + 1]
        assert nxt <= NX
        for d in range(4):
            @pl.when(has[d])
            def _(d=d):
                for x, n in used.items():
                    copy(x, d, n, opp[d]).wait_send()
        pltpu.make_async_remote_copy(
            src_ref=gat.at[pl.ds(0, nd - 1)], dst_ref=gat.at[pl.ds(0, nd - 1)], send_sem=gsend, recv_sem=grecv,
            device_id=nbr[0], device_id_type=MESH).wait_send()

    return kernel


def solution(mesh):
    nrad, nax = mesh.shape["rad"], mesh.shape["ax"]
    nd = nrad * nax
    n2 = nrad * 4
    f32 = jnp.float32

    def on_device(charge, density, previous, levels):
        vm = pl.BlockSpec(memory_space=pltpu.VMEM)
        return pl.pallas_call(
            make_kernel(nrad, nax),
            out_shape=jax.ShapeDtypeStruct(charge.shape, f32),
            in_specs=[vm, vm, vm, pl.BlockSpec(memory_space=pltpu.SMEM)],
            out_specs=vm,
            scratch_shapes=[
                pltpu.VMEM((18, 16, 128), f32),
                pltpu.VMEM((18, 16, 128), f32),
                pltpu.VMEM((6, 16, 16, 128), f32),
                pltpu.VMEM((16, 16, 128), f32),
                pltpu.VMEM((16, 16, 128), f32),
                pltpu.VMEM((8, 16, 128), f32),
                pltpu.VMEM((8, 8, 128), f32),
                pltpu.VMEM((10, 8, 128), f32),
                pltpu.VMEM((10, 8, 128), f32),
                pltpu.VMEM((6, 8, 8, 128), f32),
                pltpu.VMEM((8, 8, 128), f32),
                pltpu.VMEM((8, 8, 128), f32),
                pltpu.VMEM((NX, 4, 16, 128), f32),
                pltpu.VMEM((NX, 4, 16, 128), f32),
                pltpu.VMEM((nd, 8, 128), f32),
                pltpu.VMEM((n2 + 2, nax, 128), f32),
                pltpu.VMEM((6, n2, nax, 128), f32),
                pltpu.VMEM((n2, nax, 128), f32),
                pltpu.VMEM((n2 + 2, nax, 128), f32),
                pltpu.SemaphoreType.DMA((NX, 4)),
                pltpu.SemaphoreType.DMA((NX, 4)),
                pltpu.SemaphoreType.DMA,
                pltpu.SemaphoreType.DMA,
            ],
            compiler_params=pltpu.CompilerParams(
                collective_id=0, has_side_effects=True, vmem_limit_bytes=40 * 2**20),
        )(charge, density, previous, levels)

    return jax.shard_map(
        on_device, mesh=mesh,
        in_specs=(P("rad", "ax", None),) * 4,
        out_specs=P("rad", "ax", None), check_vma=False)
```

profile of v0, /device:TPU:1, one launch (start us, length us, event | category | flops | bytes accessed | tf_op | source)
XLA Modules:
  0.0 87.6 jit_solution(18092639748038772028)
XLA Ops:
  0.0 0.0 copy-start
  0.0 0.9 %copy-done = f32[16,16,128]{2,1,0:T(8,128)S(1)} copy-done((f32[16,16,128]{2,1,0:T(8,128)S(1)}, f32[16,16,128]{2,1,0:T(8,128)}, u32[]{:S(2)}) %copy-start) | copy-done | bytes 131096
  0.9 0.0 copy-start.1
  0.9 0.9 %copy-done.1 = f32[16,16,128]{2,1,0:T(8,128)S(1)} copy-done((f32[16,16,128]{2,1,0:T(8,128)S(1)}, f32[16,16,128]{2,1,0:T(8,128)}, u32[]{:S(2)}) %copy-start.1) | copy-done | bytes 131096
  1.8 0.0 copy-start.2
  1.8 0.9 %copy-done.2 = f32[16,16,128]{2,1,0:T(8,128)S(1)} copy-done((f32[16,16,128]{2,1,0:T(8,128)S(1)}, f32[16,16,128]{2,1,0:T(8,128)}, u32[]{:S(2)}) %copy-start.2) | copy-done | bytes 131096
  2.7 0.0 copy-start.3
  2.7 0.7 copy-done.3
  3.4 83.6 %shard_map.46 = f32[16,16,128]{2,1,0:T(8,128)S(1)} custom-call(f32[16,16,128]{2,1,0:T(8,128)S(1)} %copy-done, f32[16,16,128]{2,1,0:T(8,128)S(1)} %copy-done.1, f32[16,16,128]{2,1,0:T(8,128)S(1)} %copy-done.2, s32[1,1,8]{2,1,0:T(1,128)S(1)} %copy-done.3), custom_call_target="tpu_custom_call" | custom-call | tf_op jit(solution)/shard_map/pallas_call | solution.py:328
  87.0 0.7 copy.6
Async XLA Ops:
  0.0 0.9 %copy-start = (f32[16,16,128]{2,1,0:T(8,128)S(1)}, f32[16,16,128]{2,1,0:T(8,128)}, u32[]{:S(2)}) copy-start(f32[16,16,128]{2,1,0:T(8,128)} %charge.1) | copy-start | bytes 393220
  0.9 0.9 %copy-start.1 = (f32[16,16,128]{2,1,0:T(8,128)S(1)}, f32[16,16,128]{2,1,0:T(8,128)}, u32[]{:S(2)}) copy-start(f32[16,16,128]{2,1,0:T(8,128)} %density.1) | copy-start | bytes 393220
  1.8 0.9 %copy-start.2 = (f32[16,16,128]{2,1,0:T(8,128)S(1)}, f32[16,16,128]{2,1,0:T(8,128)}, u32[]{:S(2)}) copy-start(f32[16,16,128]{2,1,0:T(8,128)} %previous.1) | copy-start | bytes 393220
  2.7 0.7 copy-start.3
where the time goes:
time: 87.8 us; the launch traced here: 87.6 us
  Pallas kernels  83.6 us (95%)
  local copies, waits for them, and re-layouts  4.02 us (5%)
    pallas_call x1, Pallas kernels, on_device(): pl.pallas_call(make_kernel(nrad, nax), out_shape=jax.ShapeDtypeStruct(cha...  83.6 us
    unnamed x9, local copies, waits for them, and re-layouts  4.02 us

commit v1 on v0

v1 whole, which is shorter than its diff:
```python
import jax
import jax.numpy as jnp
from jax import lax
from jax.experimental import pallas as pl
from jax.experimental.pallas import tpu as pltpu
from jax.sharding import PartitionSpec as P

NU = 2
EXTRA = 2
CS = 8
PATCH = 16
MESH = pl.DeviceIdType.MESH
NX = 9
DIRS = ((-1, 0), (1, 0), (0, -1), (0, 1), (-1, -1), (1, 1), (-1, 1), (1, -1))
OPP = (1, 0, 3, 2, 5, 4, 7, 6)
H0 = 5
H1 = 6
PAD = 4


def make_kernel(nrad, nax):
    nd = nrad * nax

    def kernel(charge, density, previous, levels, out,
               de, e, ch, va, vb, vc, co, g0, d0, tmp, lv, e1, s1, m, m2, co1, h1, d1,
               gat, eg, cg, sg, f2, send_sem, recv_sem, gsend, grecv):
        ri, ai = lax.axis_index("rad"), lax.axis_index("ax")
        me = ri * nax + ai
        lo_r, hi_r, lo_a, hi_a = ri > 0, ri < nrad - 1, ai > 0, ai < nax - 1
        okr = {-1: lo_r, 1: hi_r, 0: None}
        oka = {-1: lo_a, 1: hi_a, 0: None}
        has = []
        for dr, da in DIRS:
            x, y = okr[dr], oka[da]
            has.append(y if x is None else x if y is None else jnp.logical_and(x, y))

        barrier = pltpu.get_barrier_semaphore()

        def greet(i, c):
            @pl.when(i != me)
            def _():
                pl.semaphore_signal(barrier, inc=1, device_id=(i // nax, i % nax), device_id_type=MESH)
            return c

        lax.fori_loop(0, nd, greet, 0)

        def region(dst, h, n, k, d):
            dr, da = DIRS[d]
            rows = {-1: (h - k, k), 0: (h, n), 1: (h + n, k)}[dr]
            cols = {-1: (0, 8), 0: (8, n), 1: (8 + n, 8)}[da]
            return dst.at[pl.ds(*rows), pl.ds(*cols)]

        def face(src, off, n, k, d):
            dr, da = DIRS[d]
            rows = {-1: (off[0], k), 0: (off[0], n), 1: (off[0] + n - k, k)}[dr]
            cols = {-1: (off[1], 8), 0: (off[1], n), 1: (off[1] + n - 8, 8)}[da]
            return src.at[pl.ds(*rows), pl.ds(*cols)]

        OWN0, OWN1 = (H0, 8), (H1, 8)
        plan = {
            0: (density, (0, 0), de, H0, 16, 5),
            1: (previous, (0, 0), va, H0, 16, 4),
            2: (charge, (0, 0), ch, H0, 16, 4),
            4: (e1, OWN1, e1, H1, 8, 6),
            5: (va, OWN0, vb, H0, 16, 5),
            6: (s1, OWN1, s1, H1, 8, 5),
            7: (vb, OWN0, vc, H0, 16, 4),
            8: (m, OWN1, m2, H1, 8, 6),
        }

        def copy(x, d, slot):
            dr, da = DIRS[d]
            if x == 3:
                src, dst = lv.at[8], lv.at[slot]
            else:
                source, off, dest, h, n, k = plan[x]
                src, dst = face(source, off, n, k, d), region(dest, h, n, k, slot)
            return pltpu.make_async_remote_copy(
                src_ref=src, dst_ref=dst, send_sem=send_sem.at[x, d], recv_sem=recv_sem.at[x, slot],
                device_id=(ri + dr, ai + da), device_id_type=MESH)

        def send(x):
            for d in range(8):
                @pl.when(has[d])
                def _(d=d):
                    copy(x, d, OPP[d]).start()

        def recv(x):
            for d in range(8):
                @pl.when(has[d])
                def _(d=d):
                    if x == 3:
                        copy(x, d, d).wait_recv()
                    else:
                        dest, h, n, k = plan[x][2:]
                        dst = region(dest, h, n, k, d)
                        pltpu.make_async_remote_copy(
                            src_ref=dst, dst_ref=dst, send_sem=send_sem.at[x, d], recv_sem=recv_sem.at[x, d],
                            device_id=(ri + DIRS[d][0], ai + DIRS[d][1]), device_id_type=MESH).wait_recv()

        for d in range(8):
            @pl.when(jnp.logical_not(has[d]))
            def _(d=d):
                for x, (_s, _o, dest, h, n, k) in plan.items():
                    ref = region(dest, h, n, k, d)
                    ref[...] = jnp.zeros(ref.shape, jnp.float32)
                lv[d] = jnp.zeros((8, 128), jnp.int32)

        lane8 = lax.broadcasted_iota(jnp.int32, (8, 128), 1)
        sub8 = lax.broadcasted_iota(jnp.int32, (8, 128), 0)
        lev = jnp.zeros((8, 128), jnp.int32)
        for p in range(8):
            lev = jnp.where(lane8 // PATCH == p, levels[0, 0, p], lev)
        lv[8] = lev
        pl.semaphore_wait(barrier, nd - 1)
        send(0)
        send(2)
        send(1)
        send(3)

        def inside(n):
            sub = lax.broadcasted_iota(jnp.int32, (n + 16, 128), 0)
            left, right = lo_a.astype(jnp.float32), hi_a.astype(jnp.float32)
            row = jnp.where(sub < 8, left, jnp.where(sub >= n + 8, right, 1.0))
            return [row * lo_r.astype(jnp.float32), row, row * hi_r.astype(jnp.float32)]

        def zone(r, n):
            return 0 if r < 0 else 2 if r >= n else 1

        def shifts(ref, h, r, n, step):
            c = ref[r + h]
            return c, (ref[r + h - 1], ref[r + h + 1], pltpu.roll(c, 1, 0), pltpu.roll(c, n + 15, 0),
                       pltpu.roll(c, step, 1), pltpu.roll(c, 128 - step, 1))

        def coefs(ref, h, r, n, step, scale, ins, cref, hc):
            lane = lax.broadcasted_iota(jnp.int32, (n + 16, 128), 1)
            c, (u, dn, l, rt, wl, wr) = shifts(ref, h, r, n, step)
            wl = jnp.where(lane < step, 0.0, wl)
            wr = jnp.where(lane >= 128 - step, 0.0, wr)
            t = 6.0 * c + u + dn + l + rt + wl + wr
            inv = jnp.where(ins[zone(r, n)] > 0.0, 1.0 / t, 0.0)
            cref[0, r + hc] = (c + u) * inv
            cref[1, r + hc] = (c + dn) * inv
            cref[2, r + hc] = (c + l) * inv
            cref[3, r + hc] = (c + rt) * inv
            cref[4, r + hc] = jnp.where(lane < step, 0.0, (c + wl) * inv)
            cref[5, r + hc] = jnp.where(lane >= 128 - step, 0.0, (c + wr) * inv)
            return t * (0.5 * scale), inv * (2.0 / scale)

        def update(ref, h, r, n, step, cref, hc, g):
            c, nb = shifts(ref, h, r, n, step)
            t = (g + cref[0, r + hc] * nb[0]) + cref[1, r + hc] * nb[1]
            s = cref[2, r + hc] * nb[2] + cref[3, r + hc] * nb[3]
            q = cref[4, r + hc] * nb[4] + cref[5, r + hc] * nb[5]
            return c, t + (s + q)

        def parity_of(n, step):
            return (lax.broadcasted_iota(jnp.int32, (n + 16, 128), 0)
                    + lax.broadcasted_iota(jnp.int32, (n + 16, 128), 1) // step) % 2

        def half(ref, h, n, step, cref, hc, g, colour, wide, masks=None):
            par = parity_of(n, step)
            ms = [par == colour, par == 1 - colour]
            for r in range(-wide, n + wide):
                c, new = update(ref, h, r, n, step, cref, hc, g(r))
                k = ms[r % 2]
                if masks is not None:
                    k = jnp.logical_and(k, masks[zone(r, n)])
                ref[r + h] = jnp.where(k, new, c)

        def fine(ref, colour, wide, masks=None):
            half(ref, H0, 16, 1, co, 4, lambda r: g0[r + 4], colour, wide, masks)

        def pairs(x, w):
            return x + jnp.where(lane8 % (2 * w) < w, pltpu.roll(x, 128 - w, 1), pltpu.roll(x, w, 1))

        ins0, ins1 = inside(16), inside(8)
        for r in range(16):
            e[r + H0, 8:24] = 1.0 + 0.5 * density[r]
            va[r + H0, 8:24] = previous[r]
            ch[r + H0, 8:24] = charge[r]
        for q in range(8):
            tmp[q, 0:16] = e[2 * q + H0, 8:24] + e[2 * q + 1 + H0, 8:24]
        for q in range(8):
            t = tmp[q, pl.ds(0, 8, stride=2), :] + tmp[q, pl.ds(1, 8, stride=2), :]
            e1[q + H1, 8:16] = pairs(t, 1) * 0.125
        send(4)

        recv(0)
        for r in range(-5, 21):
            z = zone(r, 16)
            for c0 in ((0, 24) if z == 1 else (0, 8, 16, 24)):
                e[r + H0, c0:c0 + 8] = ins0[z][c0:c0 + 8] * (1.0 + 0.5 * de[r + H0, c0:c0 + 8])
        recv(2)
        for r in range(-4, 20):
            dd, hh = coefs(e, H0, r, 16, 1, 1.0, ins0, co, 4)
            g0[r + 4] = ch[r + H0] * hh
            if 0 <= r < 16:
                d0[r] = dd[8:24]
        recv(1)
        for i in range(2 * NU):
            fine(va, i % 2, 3 - i)
        send(5)
        for r in range(16):
            vb[r + H0, 8:24] = va[r + H0, 8:24]
        recv(4)
        for r in range(-5, 13):
            dd, hh = coefs(e1, H1, r, 8, 2, 0.25, ins1, co1, 5)
            h1[r + 5] = hh
            if 0 <= r < 8:
                d1[r] = dd[8:16]
        recv(3)
        band = []
        for trio in ((4, 0, 6), (2, 8, 3), (7, 1, 5)):
            a, b, c = (lv[t] for t in trio)
            band.append(jnp.concatenate([a, b, b, c], axis=0))
        recv(5)
        for i in range(2 * EXTRA):
            if i % 2 == 0:
                masks = [x > i // 2 for x in band]
            fine(vb, i % 2, 4 - i, masks)
        for q in range(8):
            rs = []
            for r in (2 * q, 2 * q + 1):
                c, new = update(vb, H0, r, 16, 1, co, 4, g0[r + 4])
                rs.append(d0[r] * (new - c)[8:24])
            tmp[q, 0:16] = rs[0] + rs[1]
        for q in range(8):
            t = tmp[q, pl.ds(0, 8, stride=2), :] + tmp[q, pl.ds(1, 8, stride=2), :]
            s1[q + H1, 8:16] = pairs(t, 1) * 0.125
        send(6)
        send(7)
        recv(6)
        par = parity_of(8, 2)
        for r in range(-5, 13):
            h1[r + 5] = h1[r + 5] * s1[r + H1]
        for r in range(-4, 12):
            m[r + H1] = jnp.where(par == r % 2, h1[r + 5], 0.0)

        def middle(ref, colour, wide):
            half(ref, H1, 8, 2, co1, 5, lambda r: h1[r + 5], colour, wide)

        for i in range(1, 2 * NU):
            middle(m, i % 2, 4 - i)
        for q in range(4):
            rs = []
            for r in (2 * q, 2 * q + 1):
                c, new = update(m, H1, r, 8, 2, co1, 5, h1[r + 5])
                rs.append(d1[r] * (new - c)[8:16])
            tmp[q, 0:8] = pairs(rs[0] + rs[1], 2)
            tmp[q, 8:16] = pairs(e1[2 * q + H1, 8:16] + e1[2 * q + 1 + H1, 8:16], 2)
        lane1 = lax.broadcasted_iota(jnp.int32, (1, 128), 1)
        for k in range(2):
            for q in range(4):
                p = jnp.zeros((1, 128), jnp.float32)
                for j in range(4):
                    a = 8 * k + 2 * j
                    p = jnp.where(lane1 % 4 == j, tmp[q, a:a + 1] + tmp[q, a + 1:a + 2], p)
                gat[me, pl.ds(4 * k + q, 1)] = p * 0.125

        def gcopy(i):
            return pltpu.make_async_remote_copy(
                src_ref=gat.at[me], dst_ref=gat.at[me], send_sem=gsend, recv_sem=grecv,
                device_id=(i // nax, i % nax), device_id_type=MESH)

        def scatter(i, c):
            @pl.when(i != me)
            def _():
                gcopy(i).start()
            return c

        lax.fori_loop(0, nd, scatter, 0)
        send(8)
        everyone = pltpu.make_async_remote_copy(
            src_ref=gat.at[pl.ds(0, nd - 1)], dst_ref=gat.at[pl.ds(0, nd - 1)], send_sem=gsend, recv_sem=grecv,
            device_id=(ri, ai), device_id_type=MESH)
        everyone.wait_recv()

        n2 = nrad * 4
        zc = jnp.zeros((nax, 128), jnp.float32)
        sub = lax.broadcasted_iota(jnp.int32, (nax, 128), 0)
        lane = lax.broadcasted_iota(jnp.int32, (nax, 128), 1)
        j4 = lane % 4

        def around(c):
            lf = jnp.where(j4 == 0, pltpu.roll(pltpu.roll(c, 125, 1), 1, 0), pltpu.roll(c, 1, 1))
            rt = jnp.where(j4 == 3, pltpu.roll(pltpu.roll(c, 3, 1), nax - 1, 0), pltpu.roll(c, 127, 1))
            return lf, rt, pltpu.roll(c, 4, 1), pltpu.roll(c, 124, 1)

        first = jnp.logical_and(sub == 0, j4 == 0)
        last = jnp.logical_and(sub == nax - 1, j4 == 3)
        low = lane < 4
        high = lane >= 124
        eg[0] = zc
        eg[n2 + 1] = zc
        for r in range(n2 + 2 * PAD):
            f2[r] = zc
        for r in range(n2):
            eg[r + 1] = gat[(r // 4) * nax:(r // 4 + 1) * nax, 4 + r % 4, :]

        def coarse_coefs(r, _):
            c = eg[r + 1]
            lf, rt, wl, wr = around(c)
            lf = jnp.where(first, 0.0, lf)
            rt = jnp.where(last, 0.0, rt)
            wl = jnp.where(low, 0.0, wl)
            wr = jnp.where(high, 0.0, wr)
            u, dn = eg[r], eg[r + 2]
            t = 6.0 * c + u + dn + lf + rt + wl + wr
            h = 1.0 / t
            cg[0, r] = (c + u) * h
            cg[1, r] = (c + dn) * h
            cg[2, r] = jnp.where(first, 0.0, (c + lf) * h)
            cg[3, r] = jnp.where(last, 0.0, (c + rt) * h)
            cg[4, r] = jnp.where(low, 0.0, (c + wl) * h)
            cg[5, r] = jnp.where(high, 0.0, (c + wr) * h)
            sg[r] = h * 32.0
            return 0

        for r in range(n2):
            coarse_coefs(r, 0)
            sg[r] = sg[r] * gat[(r // 4) * nax:(r // 4 + 1) * nax, r % 4, :]
        par2 = (j4 + lane // 4) % 2

        def coarse_sweep(k, _):
            for colour in range(2):
                for r in range(n2):
                    c = f2[r + PAD]
                    lf, rt, wl, wr = around(c)
                    t = sg[r] + cg[0, r] * f2[r + PAD - 1] + cg[1, r] * f2[r + PAD + 1]
                    t = t + (cg[2, r] * lf + cg[3, r] * rt) + (cg[4, r] * wl + cg[5, r] * wr)
                    f2[r + PAD] = jnp.where(par2 == (colour + r) % 2, t, c)
            return 0

        lax.fori_loop(0, CS, coarse_sweep, 0)

        recv(8)
        m4 = lane8 % 4
        sides = ((jnp.maximum(ai - 1, 0), lo_a), (ai, None), (jnp.minimum(ai + 1, nax - 1), hi_a))
        for q in range(-3, 7):
            parts = []
            for at, ok in sides:
                own = jnp.broadcast_to(f2[4 * ri + q + PAD, pl.ds(at, 1), :], (8, 128))
                if ok is not None:
                    own = own * ok.astype(jnp.float32)
                t = jnp.zeros((8, 128), jnp.float32)
                want = sub8 // 2 - m4
                for s in range(-3, 4):
                    t = jnp.where(want == s, own if s == 0 else pltpu.roll(own, (-s) % 128, 1), t)
                parts.append(t)
            for r in (2 * q, 2 * q + 1):
                if 0 <= r < 8:
                    m2[r + H1, 0:8] = m2[r + H1, 0:8] + parts[0]
                    m2[r + H1, 8:16] = m[r + H1, 8:16] + parts[1]
                    m2[r + H1, 16:24] = m2[r + H1, 16:24] + parts[2]
                else:
                    for k in range(3):
                        m2[r + H1, 8 * k:8 * k + 8] = m2[r + H1, 8 * k:8 * k + 8] + parts[k]
        for i in range(2 * NU):
            middle(m2, i % 2, 5 - i)
        recv(7)
        for q in range(-2, 10):
            y = m2[q + H1]
            tmp[q + 2, pl.ds(0, 24, stride=2), :] = y
            tmp[q + 2, pl.ds(1, 24, stride=2), :] = y
        for r in range(-4, 20):
            t = tmp[r // 2 + 2, 8:40]
            if 0 <= r < 16:
                vc[r + H0, 0:8] = vc[r + H0, 0:8] + t[0:8]
                vc[r + H0, 8:24] = vb[r + H0, 8:24] + t[8:24]
                vc[r + H0, 24:32] = vc[r + H0, 24:32] + t[24:32]
            else:
                vc[r + H0] = vc[r + H0] + t
        for i in range(2 * NU):
            fine(vc, i % 2, 3 - i)
        out[...] = vc[H0:H0 + 16, 8:24]
        for d in range(8):
            @pl.when(has[d])
            def _(d=d):
                for x in range(NX):
                    copy(x, d, OPP[d]).wait_send()
        everyone.wait_send()

    return kernel


def solution(mesh):
    nrad, nax = mesh.shape["rad"], mesh.shape["ax"]
    nd = nrad * nax
    n2 = nrad * 4
    f32 = jnp.float32

    def on_device(charge, density, previous, levels):
        vm = pl.BlockSpec(memory_space=pltpu.VMEM)
        fine = pltpu.VMEM((16 + 2 * H0, 32, 128), f32)
        mid = pltpu.VMEM((8 + 2 * H1, 24, 128), f32)
        return pl.pallas_call(
            make_kernel(nrad, nax),
            out_shape=jax.ShapeDtypeStruct(charge.shape, f32),
            in_specs=[vm, vm, vm, pl.BlockSpec(memory_space=pltpu.SMEM)],
            out_specs=vm,
            scratch_shapes=[
                fine, fine, fine, fine, fine, fine,
                pltpu.VMEM((6, 24, 32, 128), f32),
                pltpu.VMEM((24, 32, 128), f32),
                pltpu.VMEM((16, 16, 128), f32),
                pltpu.VMEM((12, 48, 128), f32),
                pltpu.VMEM((9, 8, 128), jnp.int32),
                mid, mid, mid, mid,
                pltpu.VMEM((6, 18, 24, 128), f32),
                pltpu.VMEM((18, 24, 128), f32),
                pltpu.VMEM((8, 8, 128), f32),
                pltpu.VMEM((nd, 8, 128), f32),
                pltpu.VMEM((n2 + 2, nax, 128), f32),
                pltpu.VMEM((6, n2, nax, 128), f32),
                pltpu.VMEM((n2, nax, 128), f32),
                pltpu.VMEM((n2 + 2 * PAD, nax, 128), f32),
                pltpu.SemaphoreType.DMA((NX, 8)),
                pltpu.SemaphoreType.DMA((NX, 8)),
                pltpu.SemaphoreType.DMA,
                pltpu.SemaphoreType.DMA,
            ],
            compiler_params=pltpu.CompilerParams(
                collective_id=0, has_side_effects=True, vmem_limit_bytes=40 * 2**20),
        )(charge, density, previous, levels)

    return jax.shard_map(
        on_device, mesh=mesh,
        in_specs=(P("rad", "ax", None),) * 4,
        out_specs=P("rad", "ax", None), check_vma=False)
```

time: 87.8 us -> 52.1 us (0.59)
  Pallas kernels: 83.6 us -> 47.6 us
    pallas_call x1, Pallas kernels: 83.6 us -> 47.6 us  [on_device(): pl.pallas_call(make_kernel(nrad, nax), out_shape=jax.ShapeDtypeStruct(cha...]
where the time goes in v1:
time: 52.1 us; the launch traced here: 51.6 us
  Pallas kernels  47.6 us (91%)
  local copies, waits for them, and re-layouts  4.02 us (8%)
    pallas_call x1, Pallas kernels, on_device(): pl.pallas_call(make_kernel(nrad, nax), out_shape=jax.ShapeDtypeStruct(cha...  47.6 us
    unnamed x9, local copies, waits for them, and re-layouts  4.02 us

profile of v1, /device:TPU:1, one launch (start us, length us, event | category | flops | bytes accessed | tf_op | source)
XLA Modules:
  0.0 51.6 jit_solution(5975583837144041083)
XLA Ops:
  0.0 0.0 copy-start
  0.0 0.9 %copy-done = f32[16,16,128]{2,1,0:T(8,128)S(1)} copy-done((f32[16,16,128]{2,1,0:T(8,128)S(1)}, f32[16,16,128]{2,1,0:T(8,128)}, u32[]{:S(2)}) %copy-start) | copy-done | bytes 131096
  0.9 0.0 copy-start.1
  0.9 0.9 %copy-done.1 = f32[16,16,128]{2,1,0:T(8,128)S(1)} copy-done((f32[16,16,128]{2,1,0:T(8,128)S(1)}, f32[16,16,128]{2,1,0:T(8,128)}, u32[]{:S(2)}) %copy-start.1) | copy-done | bytes 131096
  1.8 0.0 copy-start.2
  1.8 0.9 %copy-done.2 = f32[16,16,128]{2,1,0:T(8,128)S(1)} copy-done((f32[16,16,128]{2,1,0:T(8,128)S(1)}, f32[16,16,128]{2,1,0:T(8,128)}, u32[]{:S(2)}) %copy-start.2) | copy-done | bytes 131096
  2.7 0.0 copy-start.3
  2.7 0.7 %copy-done.3 = s32[1,1,8]{2,1,0:T(1,128)S(1)} copy-done((s32[1,1,8]{2,1,0:T(1,128)S(1)}, s32[1,1,8]{2,1,0:T(1,128)}, u32[]{:S(2)}) %copy-start.3) | copy-done | bytes 56
  3.4 47.6 %shard_map.46 = f32[16,16,128]{2,1,0:T(8,128)S(1)} custom-call(f32[16,16,128]{2,1,0:T(8,128)S(1)} %copy-done, f32[16,16,128]{2,1,0:T(8,128)S(1)} %copy-done.1, f32[16,16,128]{2,1,0:T(8,128)S(1)} %copy-done.2, s32[1,1,8]{2,1,0:T(1,128)S(1)} %copy-done.3), custom_call_target="tpu_custom_call" | custom-call | tf_op jit(solution)/shard_map/pallas_call | solution.py:397
  51.0 0.7 %copy.6 = f32[16,16,128]{2,1,0:T(8,128)} copy(f32[16,16,128]{2,1,0:T(8,128)S(1)} %shard_map.46) | data formatting | bytes 262144
Async XLA Ops:
  0.0 0.9 %copy-start = (f32[16,16,128]{2,1,0:T(8,128)S(1)}, f32[16,16,128]{2,1,0:T(8,128)}, u32[]{:S(2)}) copy-start(f32[16,16,128]{2,1,0:T(8,128)} %charge.1) | copy-start | bytes 393220
  0.9 0.9 %copy-start.1 = (f32[16,16,128]{2,1,0:T(8,128)S(1)}, f32[16,16,128]{2,1,0:T(8,128)}, u32[]{:S(2)}) copy-start(f32[16,16,128]{2,1,0:T(8,128)} %density.1) | copy-start | bytes 393220
  1.8 0.9 %copy-start.2 = (f32[16,16,128]{2,1,0:T(8,128)S(1)}, f32[16,16,128]{2,1,0:T(8,128)}, u32[]{:S(2)}) copy-start(f32[16,16,128]{2,1,0:T(8,128)} %previous.1) | copy-start | bytes 393220
  2.7 0.7 %copy-start.3 = (s32[1,1,8]{2,1,0:T(1,128)S(1)}, s32[1,1,8]{2,1,0:T(1,128)}, u32[]{:S(2)}) copy-start(s32[1,1,8]{2,1,0:T(1,128)} %levels.1) | copy-start | bytes 100

commit v2 on v1

--- a/solution.py
+++ b/solution.py
@@ -23,7 +23,7 @@
 
     def kernel(charge, density, previous, levels, out,
                de, e, ch, va, vb, vc, co, g0, d0, tmp, lv, e1, s1, m, m2, co1, h1, d1,
-               gat, eg, cg, sg, f2, send_sem, recv_sem, gsend, grecv):
+               pv, pt, pe, ps, pm, ssd, rsd, gat, eg, cg, sg, f2, send_sem, recv_sem, gsend, grecv):
         ri, ai = lax.axis_index("rad"), lax.axis_index("ax")
         me = ri * nax + ai
         lo_r, hi_r, lo_a, hi_a = ri > 0, ri < nrad - 1, ai > 0, ai < nax - 1
@@ -44,37 +44,46 @@
 
         lax.fori_loop(0, nd, greet, 0)
 
-        def region(dst, h, n, k, d):
-            dr, da = DIRS[d]
-            rows = {-1: (h - k, k), 0: (h, n), 1: (h + n, k)}[dr]
-            cols = {-1: (0, 8), 0: (8, n), 1: (8 + n, 8)}[da]
-            return dst.at[pl.ds(*rows), pl.ds(*cols)]
-
-        def face(src, off, n, k, d):
-            dr, da = DIRS[d]
-            rows = {-1: (off[0], k), 0: (off[0], n), 1: (off[0] + n - k, k)}[dr]
-            cols = {-1: (off[1], 8), 0: (off[1], n), 1: (off[1] + n - 8, 8)}[da]
-            return src.at[pl.ds(*rows), pl.ds(*cols)]
-
-        OWN0, OWN1 = (H0, 8), (H1, 8)
         plan = {
-            0: (density, (0, 0), de, H0, 16, 5),
-            1: (previous, (0, 0), va, H0, 16, 4),
-            2: (charge, (0, 0), ch, H0, 16, 4),
-            4: (e1, OWN1, e1, H1, 8, 6),
-            5: (va, OWN0, vb, H0, 16, 5),
-            6: (s1, OWN1, s1, H1, 8, 5),
-            7: (vb, OWN0, vc, H0, 16, 4),
-            8: (m, OWN1, m2, H1, 8, 6),
+            0: (density, (0, 0), de, H0, 16, 16, 5),
+            1: (pv, (0, 0), pt, 2, 8, 16, 2),
+            2: (charge, (0, 0), ch, H0, 16, 16, 4),
+            4: (pe, (3, 8), pe, 3, 4, 8, 3),
+            5: (va, (H0, 8), vb, H0, 16, 16, 5),
+            6: (ps, (3, 8), ps, 3, 4, 8, 3),
+            7: (vb, (H0, 8), vc, H0, 16, 16, 4),
+            8: (pm, (3, 8), pm, 3, 4, 8, 3),
         }
-
-        def copy(x, d, slot):
+        side = {1: (0, 1, 4, 1), 2: (1, 2, 8, 2), 7: (2, 2, 8, 2)}
+
+        def dest(x, d):
             dr, da = DIRS[d]
             if x == 3:
-                src, dst = lv.at[8], lv.at[slot]
-            else:
-                source, off, dest, h, n, k = plan[x]
-                src, dst = face(source, off, n, k, d), region(dest, h, n, k, slot)
+                return lv.at[d]
+            if x in side and da:
+                t, h, n, k = side[x]
+                rows = {-1: (h - k, k), 0: (h, n), 1: (h + n, k)}[dr]
+                return rsd.at[t, (da + 1) // 2, pl.ds(*rows)]
+            tile, h, n, w, k = plan[x][2:]
+            rows = {-1: (h - k, k), 0: (h, n), 1: (h + n, k)}[dr]
+            cols = {-1: (0, 8), 0: (8, w), 1: (8 + w, 8)}[da]
+            return tile.at[pl.ds(*rows), pl.ds(*cols)]
+
+        def origin(x, d):
+            dr, da = DIRS[d]
+            if x == 3:
+                return lv.at[8]
+            if x in side and da:
+                t, h, n, k = side[x]
+                rows = {-1: (0, k), 0: (0, n), 1: (n - k, k)}[dr]
+                return ssd.at[t, (da + 1) // 2, pl.ds(*rows)]
+            src, off, _tile, h, n, w, k = plan[x]
+            rows = {-1: (off[0], k), 0: (off[0], n), 1: (off[0] + n - k, k)}[dr]
+            cols = {-1: (off[1], 8), 0: (off[1], w), 1: (off[1] + w - 8, 8)}[da]
+            return src.at[pl.ds(*rows), pl.ds(*cols)]
+
+        def copy(x, d, src, dst, slot):
+            dr, da = DIRS[d]
             return pltpu.make_async_remote_copy(
                 src_ref=src, dst_ref=dst, send_sem=send_sem.at[x, d], recv_sem=recv_sem.at[x, slot],
                 device_id=(ri + dr, ai + da), device_id_type=MESH)
@@ -83,28 +92,20 @@
             for d in range(8):
                 @pl.when(has[d])
                 def _(d=d):
-                    copy(x, d, OPP[d]).start()
+                    copy(x, d, origin(x, d), dest(x, OPP[d]), OPP[d]).start()
 
         def recv(x):
             for d in range(8):
                 @pl.when(has[d])
                 def _(d=d):
-                    if x == 3:
-                        copy(x, d, d).wait_recv()
-                    else:
-                        dest, h, n, k = plan[x][2:]
-                        dst = region(dest, h, n, k, d)
-                        pltpu.make_async_remote_copy(
-                            src_ref=dst, dst_ref=dst, send_sem=send_sem.at[x, d], recv_sem=recv_sem.at[x, d],
-                            device_id=(ri + DIRS[d][0], ai + DIRS[d][1]), device_id_type=MESH).wait_recv()
+                    copy(x, d, dest(x, d), dest(x, d), d).wait_recv()
 
         for d in range(8):
             @pl.when(jnp.logical_not(has[d]))
             def _(d=d):
-                for x, (_s, _o, dest, h, n, k) in plan.items():
-                    ref = region(dest, h, n, k, d)
-                    ref[...] = jnp.zeros(ref.shape, jnp.float32)
-                lv[d] = jnp.zeros((8, 128), jnp.int32)
+                for x in range(NX):
+                    ref = dest(x, d)
+                    ref[...] = jnp.zeros(ref.shape, ref.dtype)
 
         lane8 = lax.broadcasted_iota(jnp.int32, (8, 128), 1)
         sub8 = lax.broadcasted_iota(jnp.int32, (8, 128), 0)
@@ -112,6 +113,41 @@
         for p in range(8):
             lev = jnp.where(lane8 // PATCH == p, levels[0, 0, p], lev)
         lv[8] = lev
+
+        def pack_sides(x, get):
+            t, h, n, k = side[x]
+            for q in range(n):
+                a, b = get(2 * q), get(2 * q + 1)
+                ssd[t, 0, q] = jnp.where(sub8 < 4, a[0:8], pltpu.roll(b[0:8], 4, 0))
+                ssd[t, 1, q] = jnp.where(sub8 < 4, pltpu.roll(a[8:16], 4, 0), b[8:16])
+
+        def unpack_sides(x, ref, off):
+            t, h, n, k = side[x]
+            for q in range(-k, n + k):
+                a, b = rsd[t, 0, q + h], rsd[t, 1, q + h]
+                ref[2 * q + off, 0:8] = pltpu.roll(a, 4, 0)
+                ref[2 * q + 1 + off, 0:8] = a
+                ref[2 * q + off, 24:32] = b
+                ref[2 * q + 1 + off, 24:32] = pltpu.roll(b, 4, 0)
+
+        def pack_rows(ref, q, a, b):
+            ref[q + 3, 8:16] = jnp.where(lane8 % 2 == 0, a, b)
+
+        lane24 = lax.broadcasted_iota(jnp.int32, (24, 128), 1)
+
+        def unpack_rows(ref, dst):
+            for q in range(-3, 7):
+                p = ref[q + 3]
+                dst[2 * q + H1] = jnp.where(lane24 % 2 == 0, p, pltpu.roll(p, 1, 1))
+                dst[2 * q + 1 + H1] = jnp.where(lane24 % 2 == 0, pltpu.roll(p, 127, 1), p)
+
+        odd16 = (lax.broadcasted_iota(jnp.int32, (16, 128), 0) + lax.broadcasted_iota(jnp.int32, (16, 128), 1)) % 2 == 1
+        for q in range(8):
+            p = jnp.where(odd16, previous[2 * q], previous[2 * q + 1])
+            pv[q] = p
+            pt[q + 2, 8:24] = p
+        pack_sides(1, lambda q: pv[q])
+        pack_sides(2, lambda r: charge[r])
         pl.semaphore_wait(barrier, nd - 1)
         send(0)
         send(2)
@@ -177,14 +213,12 @@
         ins0, ins1 = inside(16), inside(8)
         for r in range(16):
             e[r + H0, 8:24] = 1.0 + 0.5 * density[r]
-            va[r + H0, 8:24] = previous[r]
             ch[r + H0, 8:24] = charge[r]
         for q in range(8):
             tmp[q, 0:16] = e[2 * q + H0, 8:24] + e[2 * q + 1 + H0, 8:24]
-        for q in range(8):
-            t = tmp[q, pl.ds(0, 8, stride=2), :] + tmp[q, pl.ds(1, 8, stride=2), :]
-            e1[q + H1, 8:16] = pairs(t, 1) * 0.125
-        send(4)
+        for q in range(4):
+            t = [tmp[p, pl.ds(0, 8, stride=2), :] + tmp[p, pl.ds(1, 8, stride=2), :] for p in (2 * q, 2 * q + 1)]
+            pack_rows(pe, q, pairs(t[0], 1) * 0.125, pairs(t[1], 1) * 0.125)
 
         recv(0)
         for r in range(-5, 21):
@@ -192,18 +226,25 @@
             for c0 in ((0, 24) if z == 1 else (0, 8, 16, 24)):
                 e[r + H0, c0:c0 + 8] = ins0[z][c0:c0 + 8] * (1.0 + 0.5 * de[r + H0, c0:c0 + 8])
         recv(2)
+        unpack_sides(2, ch, H0)
         for r in range(-4, 20):
             dd, hh = coefs(e, H0, r, 16, 1, 1.0, ins0, co, 4)
             g0[r + 4] = ch[r + H0] * hh
             if 0 <= r < 16:
                 d0[r] = dd[8:24]
         recv(1)
+        send(4)
+        unpack_sides(1, pt, 2)
+        for q in range(-2, 10):
+            va[2 * q + H0] = pt[q + 2]
+            va[2 * q + 1 + H0] = pt[q + 2]
         for i in range(2 * NU):
             fine(va, i % 2, 3 - i)
         send(5)
         for r in range(16):
             vb[r + H0, 8:24] = va[r + H0, 8:24]
         recv(4)
+        unpack_rows(pe, e1)
         for r in range(-5, 13):
             dd, hh = coefs(e1, H1, r, 8, 2, 0.25, ins1, co1, 5)
             h1[r + 5] = hh
@@ -225,12 +266,14 @@
                 c, new = update(vb, H0, r, 16, 1, co, 4, g0[r + 4])
                 rs.append(d0[r] * (new - c)[8:24])
             tmp[q, 0:16] = rs[0] + rs[1]
-        for q in range(8):
-            t = tmp[q, pl.ds(0, 8, stride=2), :] + tmp[q, pl.ds(1, 8, stride=2), :]
-            s1[q + H1, 8:16] = pairs(t, 1) * 0.125
+        for q in range(4):
+            t = [tmp[p, pl.ds(0, 8, stride=2), :] + tmp[p, pl.ds(1, 8, stride=2), :] for p in (2 * q, 2 * q + 1)]
+            pack_rows(ps, q, pairs(t[0], 1) * 0.125, pairs(t[1], 1) * 0.125)
         send(6)
+        pack_sides(7, lambda r: vb[r + H0, 8:24])
+        recv(6)
         send(7)
-        recv(6)
+        unpack_rows(ps, s1)
         par = parity_of(8, 2)
         for r in range(-5, 13):
             h1[r + 5] = h1[r + 5] * s1[r + H1]
@@ -270,6 +313,8 @@
             return c
 
         lax.fori_loop(0, nd, scatter, 0)
+        for q in range(4):
+            pack_rows(pm, q, m[2 * q + H1, 8:16], m[2 * q + 1 + H1, 8:16])
         send(8)
         everyone = pltpu.make_async_remote_copy(
             src_ref=gat.at[pl.ds(0, nd - 1)], dst_ref=gat.at[pl.ds(0, nd - 1)], send_sem=gsend, recv_sem=grecv,
@@ -335,6 +380,7 @@
         lax.fori_loop(0, CS, coarse_sweep, 0)
 
         recv(8)
+        unpack_rows(pm, m2)
         m4 = lane8 % 4
         sides = ((jnp.maximum(ai - 1, 0), lo_a), (ai, None), (jnp.minimum(ai + 1, nax - 1), hi_a))
         for q in range(-3, 7):
@@ -349,16 +395,12 @@
                     t = jnp.where(want == s, own if s == 0 else pltpu.roll(own, (-s) % 128, 1), t)
                 parts.append(t)
             for r in (2 * q, 2 * q + 1):
-                if 0 <= r < 8:
-                    m2[r + H1, 0:8] = m2[r + H1, 0:8] + parts[0]
-                    m2[r + H1, 8:16] = m[r + H1, 8:16] + parts[1]
-                    m2[r + H1, 16:24] = m2[r + H1, 16:24] + parts[2]
-                else:
-                    for k in range(3):
-                        m2[r + H1, 8 * k:8 * k + 8] = m2[r + H1, 8 * k:8 * k + 8] + parts[k]
+                for k in range(3):
+                    m2[r + H1, 8 * k:8 * k + 8] = m2[r + H1, 8 * k:8 * k + 8] + parts[k]
         for i in range(2 * NU):
             middle(m2, i % 2, 5 - i)
         recv(7)
+        unpack_sides(7, vc, H0)
         for q in range(-2, 10):
             y = m2[q + H1]
             tmp[q + 2, pl.ds(0, 24, stride=2), :] = y
@@ -378,7 +420,7 @@
             @pl.when(has[d])
             def _(d=d):
                 for x in range(NX):
-                    copy(x, d, OPP[d]).wait_send()
+                    copy(x, d, origin(x, d), origin(x, d), OPP[d]).wait_send()
         everyone.wait_send()
 
     return kernel
@@ -394,6 +436,7 @@
         vm = pl.BlockSpec(memory_space=pltpu.VMEM)
         fine = pltpu.VMEM((16 + 2 * H0, 32, 128), f32)
         mid = pltpu.VMEM((8 + 2 * H1, 24, 128), f32)
+        pack = pltpu.VMEM((10, 24, 128), f32)
         return pl.pallas_call(
             make_kernel(nrad, nax),
             out_shape=jax.ShapeDtypeStruct(charge.shape, f32),
@@ -410,6 +453,11 @@
                 pltpu.VMEM((6, 18, 24, 128), f32),
                 pltpu.VMEM((18, 24, 128), f32),
                 pltpu.VMEM((8, 8, 128), f32),
+                pltpu.VMEM((8, 16, 128), f32),
+                pltpu.VMEM((12, 32, 128), f32),
+                pack, pack, pack,
+                pltpu.VMEM((3, 2, 8, 8, 128), f32),
+                pltpu.VMEM((3, 2, 12, 8, 128), f32),
                 pltpu.VMEM((nd, 8, 128), f32),
                 pltpu.VMEM((n2 + 2, nax, 128), f32),
                 pltpu.VMEM((6, n2, nax, 128), f32),

time: 52.1 us -> 44.2 us (0.85)
  Pallas kernels: 47.6 us -> 40 us
    pallas_call x1, Pallas kernels: 47.6 us -> 40 us  [on_device(): pl.pallas_call(make_kernel(nrad, nax), out_shape=jax.ShapeDtypeStruct(cha...]
where the time goes in v2:
time: 44.2 us; the launch traced here: 44.1 us
  Pallas kernels  40 us (90%)
  local copies, waits for them, and re-layouts  4.02 us (9%)
    pallas_call x1, Pallas kernels, on_device(): pl.pallas_call(make_kernel(nrad, nax), out_shape=jax.ShapeDtypeStruct(cha...  40 us
    unnamed x9, local copies, waits for them, and re-layouts  4.02 us

profile of v2, /device:TPU:1, one launch (start us, length us, event | category | flops | bytes accessed | tf_op | source)
XLA Modules:
  0.0 44.1 jit_solution(14010778286546183088)
XLA Ops:
  0.0 0.0 copy-start
  0.0 0.9 %copy-done = f32[16,16,128]{2,1,0:T(8,128)S(1)} copy-done((f32[16,16,128]{2,1,0:T(8,128)S(1)}, f32[16,16,128]{2,1,0:T(8,128)}, u32[]{:S(2)}) %copy-start) | copy-done | bytes 131096
  0.9 0.0 copy-start.1
  0.9 0.9 %copy-done.1 = f32[16,16,128]{2,1,0:T(8,128)S(1)} copy-done((f32[16,16,128]{2,1,0:T(8,128)S(1)}, f32[16,16,128]{2,1,0:T(8,128)}, u32[]{:S(2)}) %copy-start.1) | copy-done | bytes 131096
  1.8 0.0 copy-start.2
  1.8 0.9 %copy-done.2 = f32[16,16,128]{2,1,0:T(8,128)S(1)} copy-done((f32[16,16,128]{2,1,0:T(8,128)S(1)}, f32[16,16,128]{2,1,0:T(8,128)}, u32[]{:S(2)}) %copy-start.2) | copy-done | bytes 131096
  2.7 0.0 copy-start.3
  2.7 0.7 %copy-done.3 = s32[1,1,8]{2,1,0:T(1,128)S(1)} copy-done((s32[1,1,8]{2,1,0:T(1,128)S(1)}, s32[1,1,8]{2,1,0:T(1,128)}, u32[]{:S(2)}) %copy-start.3) | copy-done | bytes 56
  3.4 40.0 %shard_map.46 = f32[16,16,128]{2,1,0:T(8,128)S(1)} custom-call(f32[16,16,128]{2,1,0:T(8,128)S(1)} %copy-done, f32[16,16,128]{2,1,0:T(8,128)S(1)} %copy-done.1, f32[16,16,128]{2,1,0:T(8,128)S(1)} %copy-done.2, s32[1,1,8]{2,1,0:T(1,128)S(1)} %copy-done.3), custom_call_target="tpu_custom_call" | custom-call | tf_op jit(solution)/shard_map/pallas_call | solution.py:440
  43.4 0.7 %copy.6 = f32[16,16,128]{2,1,0:T(8,128)} copy(f32[16,16,128]{2,1,0:T(8,128)S(1)} %shard_map.46) | data formatting | bytes 262144
Async XLA Ops:
  0.0 0.9 %copy-start = (f32[16,16,128]{2,1,0:T(8,128)S(1)}, f32[16,16,128]{2,1,0:T(8,128)}, u32[]{:S(2)}) copy-start(f32[16,16,128]{2,1,0:T(8,128)} %charge.1) | copy-start | bytes 393220
  0.9 0.9 %copy-start.1 = (f32[16,16,128]{2,1,0:T(8,128)S(1)}, f32[16,16,128]{2,1,0:T(8,128)}, u32[]{:S(2)}) copy-start(f32[16,16,128]{2,1,0:T(8,128)} %density.1) | copy-start | bytes 393220
  1.8 0.9 %copy-start.2 = (f32[16,16,128]{2,1,0:T(8,128)S(1)}, f32[16,16,128]{2,1,0:T(8,128)}, u32[]{:S(2)}) copy-start(f32[16,16,128]{2,1,0:T(8,128)} %previous.1) | copy-start | bytes 393220
  2.7 0.7 %copy-start.3 = (s32[1,1,8]{2,1,0:T(1,128)S(1)}, s32[1,1,8]{2,1,0:T(1,128)}, u32[]{:S(2)}) copy-start(s32[1,1,8]{2,1,0:T(1,128)} %levels.1) | copy-start | bytes 100

commit v3 on v2

--- a/solution.py
+++ b/solution.py
@@ -21,7 +21,7 @@
 def make_kernel(nrad, nax):
     nd = nrad * nax
 
-    def kernel(charge, density, previous, levels, out,
+    def kernel(charge_in, density_in, previous_in, levels_in, out, charge, density, previous, levels, lsem,
                de, e, ch, va, vb, vc, co, g0, d0, tmp, lv, e1, s1, m, m2, co1, h1, d1,
                pv, pt, pe, ps, pm, ssd, rsd, gat, eg, cg, sg, f2, send_sem, recv_sem, gsend, grecv):
         ri, ai = lax.axis_index("rad"), lax.axis_index("ax")
@@ -34,6 +34,10 @@
             x, y = okr[dr], oka[da]
             has.append(y if x is None else x if y is None else jnp.logical_and(x, y))
 
+        loads = [pltpu.make_async_copy(a, b, lsem.at[i]) for i, (a, b) in enumerate((
+            (previous_in, previous), (charge_in, charge), (density_in, density), (levels_in, levels)))]
+        for c in loads:
+            c.start()
         barrier = pltpu.get_barrier_semaphore()
 
         def greet(i, c):
@@ -107,6 +111,8 @@
                     ref = dest(x, d)
                     ref[...] = jnp.zeros(ref.shape, ref.dtype)
 
+        for c in loads:
+            c.wait()
         lane8 = lax.broadcasted_iota(jnp.int32, (8, 128), 1)
         sub8 = lax.broadcasted_iota(jnp.int32, (8, 128), 0)
         lev = jnp.zeros((8, 128), jnp.int32)
@@ -440,9 +446,14 @@
         return pl.pallas_call(
             make_kernel(nrad, nax),
             out_shape=jax.ShapeDtypeStruct(charge.shape, f32),
-            in_specs=[vm, vm, vm, pl.BlockSpec(memory_space=pltpu.SMEM)],
+            in_specs=[pl.BlockSpec(memory_space=pltpu.HBM)] * 4,
             out_specs=vm,
             scratch_shapes=[
+                pltpu.VMEM((16, 16, 128), f32),
+                pltpu.VMEM((16, 16, 128), f32),
+                pltpu.VMEM((16, 16, 128), f32),
+                pltpu.SMEM((1, 1, 8), jnp.int32),
+                pltpu.SemaphoreType.DMA((4,)),
                 fine, fine, fine, fine, fine, fine,
                 pltpu.VMEM((6, 24, 32, 128), f32),
                 pltpu.VMEM((24, 32, 128), f32),
@@ -469,7 +480,7 @@
                 pltpu.SemaphoreType.DMA,
             ],
             compiler_params=pltpu.CompilerParams(
-                collective_id=0, has_side_effects=True, vmem_limit_bytes=40 * 2**20),
+                collective_id=0, has_side_effects=True, vmem_limit_bytes=64 * 2**20),
         )(charge, density, previous, levels)
 
     return jax.shard_map(

time: 44.2 us -> 41.8 us (0.946)
  local copies, waits for them, and re-layouts: 4.02 us -> 1.57 us
    unnamed x9 -> x1, local copies, waits for them, and re-layouts: 4.02 us -> 1.57 us
where the time goes in v3:
time: 41.8 us; the launch traced here: 41.6 us
  Pallas kernels  40 us (96%)
  local copies, waits for them, and re-layouts  1.57 us (4%)
    pallas_call x1, Pallas kernels, on_device(): pl.pallas_call(make_kernel(nrad, nax), out_shape=jax.ShapeDtypeStruct(cha...  40 us
    unnamed x1, local copies, waits for them, and re-layouts  1.57 us

profile of v3, /device:TPU:1, one launch (start us, length us, event | category | flops | bytes accessed | tf_op | source)
XLA Modules:
  0.0 41.6 jit_solution(18217746124831259838)
XLA Ops:
  0.0 40.0 %shard_map.46 = f32[16,16,128]{2,1,0:T(8,128)} custom-call(f32[16,16,128]{2,1,0:T(8,128)} %charge_in.1, f32[16,16,128]{2,1,0:T(8,128)} %density_in.1, f32[16,16,128]{2,1,0:T(8,128)} %previous_in.1, s32[1,1,8]{2,1,0:T(1,128)} %levels_in.1), custom_call_target="tpu_custom_call" | custom-call | tf_op jit(solution)/shard_map/pallas_call | solution.py:446
  40.1 1.6 %copy.6 = f32[16,16,128]{2,1,0:T(8,128)} copy(f32[16,16,128]{2,1,0:T(8,128)} %shard_map.46) | data formatting | bytes 262144
